TPU v7x, 512 devices: a whole 4x4x16 slice. The times are simulated.
512 devices in a mesh: row: 16 (over y, x_lo, core), col: 32 (over z, x_hi).
Axes of the slice: x: 4 (x_hi: 2, x_lo: 2; x = x_hi * 2 + x_lo), y: 4, z: 16, core: 2. Of those that a mesh axis runs over, the one named last changes fastest.
Arguments:
- object_field: float32 [2, 4096, 8192], P(None, 'row', 'col'), may hold values from -6 to 6
- probe: float32 [2, 256, 256], replicated, may hold values from -6 to 6
- counts_measured: float32 [16, 32, 4, 256, 256], P('row', 'col'), may hold values from 0.05 to 6
- offsets: int32 [16, 32, 4, 2], P('row', 'col'), may hold values from 0 to 255
- slot_count: int32 [16, 32], P('row', 'col'), may hold values from 1 to 4, as said below
Outputs:
- object_grad: float32 [2, 4096, 8192], P(None, 'row', 'col')
- probe_step: float32 [2, 256, 256], replicated
Inputs may be any that keep to these rules, and one draw needn't show every extreme that they name: `slot_count`: of the two tiles (a, b) and (a, b + 16) one lists more than 2 positions and the other fewer than 2; some tile lists 4. Offsets lie inside the tile; slots at or beyond a tile's count hold offsets too but are not used.
All inputs are finite; a program needn't handle non-finite values.
Results may differ from a plain program's by a relative error of at most 0.0003.
Values sent between devices are 32-bit elements; how exact they have to be, the bound alone decides.
A program may use at most 192 MiB of HBM per device.

v0:
```python
import math

import jax
import jax.numpy as jnp
from jax import lax
from jax.sharding import PartitionSpec as P


def passed_along(block, axis, distance):
    devices = range(lax.axis_size(axis))
    route = [(i - distance, i) for i in devices if i - distance in devices]
    return lax.ppermute(block, axis, route)


def dft_tables(size):
    steps = jnp.arange(size, dtype=jnp.int32)
    product = steps[:, None] * steps[None, :] % size
    angle = product.astype(jnp.float32) * (2.0 * math.pi / size)
    scale = 1.0 / math.sqrt(size)
    return (jnp.cos(angle) * scale, -jnp.sin(angle) * scale)


def matmul(left, right):
    return jnp.dot(left, right, precision=lax.Precision.HIGHEST, preferred_element_type=jnp.float32)


def transform(real_part, imag_part, table_re, table_im):
    left_re = matmul(table_re, real_part) - matmul(table_im, imag_part)
    left_im = matmul(table_re, imag_part) + matmul(table_im, real_part)
    out_re = matmul(left_re, table_re) - matmul(left_im, table_im)
    out_im = matmul(left_re, table_im) + matmul(left_im, table_re)
    return (out_re, out_im)


def process(patch, measured, probe, table_re, table_im):
    exit_re = probe[0] * patch[0] - probe[1] * patch[1]
    exit_im = probe[0] * patch[1] + probe[1] * patch[0]
    wave_re, wave_im = transform(exit_re, exit_im, table_re, table_im)
    model = wave_re * wave_re + wave_im * wave_im + 0.5
    weight = 1.0 - measured / model
    chi_re, chi_im = transform(weight * wave_re, weight * wave_im, table_re, -table_im)
    gpatch = jnp.stack(
        [probe[0] * chi_re + probe[1] * chi_im, probe[0] * chi_im - probe[1] * chi_re]
    )
    gterm = jnp.stack(
        [patch[0] * chi_re + patch[1] * chi_im, patch[0] * chi_im - patch[1] * chi_re]
    )
    illum = patch[0] * patch[0] + patch[1] * patch[1]
    return (gpatch, gterm, illum)


def on_device(object_field, probe, counts_measured, offsets, slot_count):
    tile = object_field.shape[1]
    size = probe.shape[1]
    table_re, table_im = dft_tables(size)
    lower = passed_along(object_field, "row", -1)
    column = jnp.concatenate([object_field, lower], axis=1)
    right = passed_along(column, "col", -1)
    extended = jnp.concatenate([column, right], axis=2)
    measured_all = counts_measured[0, 0]
    offs = offsets[0, 0]
    count = slot_count[0, 0]
    zero = jnp.int32(0)

    def take(offset_pair):
        return lax.dynamic_slice(extended, (zero, offset_pair[0], offset_pair[1]), (2, size, size))

    def place(grad_ext, offset_pair, gpatch):
        current = lax.dynamic_slice(
            grad_ext, (zero, offset_pair[0], offset_pair[1]), (2, size, size)
        )
        return lax.dynamic_update_slice(
            grad_ext, current + gpatch, (zero, offset_pair[0], offset_pair[1])
        )

    def own_step(index, carry):
        grad_ext, gprobe, illum = carry
        gpatch, gterm, ill = process(
            take(offs[index]), measured_all[index], probe, table_re, table_im
        )
        return (place(grad_ext, offs[index], gpatch), gprobe + gterm, illum + ill)

    init = (
        jnp.zeros_like(extended),
        jnp.zeros((2, size, size), jnp.float32),
        jnp.zeros((size, size), jnp.float32),
    )
    grad_ext, gprobe, illum = lax.fori_loop(0, count, own_step, init)
    from_left = passed_along(grad_ext[:, :, tile:], "col", 1)
    strip = grad_ext[:, :, :tile] + from_left
    from_above = passed_along(strip[:, tile:, :], "row", 1)
    object_grad = strip[:, :tile, :] + from_above
    total_probe, total_illum = lax.psum((gprobe, illum), ("row", "col"))
    probe_step = total_probe / jnp.sqrt(total_illum + 1.0)
    return (object_grad, probe_step)


def solution(mesh):
    return jax.shard_map(
        on_device,
        mesh=mesh,
        in_specs=(
            P(None, "row", "col"),
            P(),
            P("row", "col", None, None, None),
            P("row", "col", None, None),
            P("row", "col"),
        ),
        out_specs=(P(None, "row", "col"), P()),
        check_vma=False,
    )
```

profile of v0, /device:TPU:1, one launch (start us, length us, event | category | flops | bytes accessed | tf_op | source)
XLA Modules:
  0.0 696.0 jit_solution(18166990997421391397)
XLA Ops:
  7.2 8.8 %collective-permute-start = (f32[2,256,256]{2,1,0:T(8,128)}, f32[2,256,256]{2,1,0:T(8,128)S(1)}, u32[]{:S(2)}, u32[]{:S(2)}) collective-permute-start(f32[2,256,256]{2,1,0:T(8,128)} %param.7), channel_id=1, source_target_pairs={{32,0},{64,32},{96,64},{128,96},{160,128},{192,160},{224,192},{256... | collective-permute-start | bytes 1572872 | tf_op jit(solution)/shard_map/ppermute | solution.py:12
  17.1 1.7 collective-permute-done
  20.1 26.9 %collective-permute-done.1 = f32[2,512,256]{2,1,0:T(8,128)} collective-permute-done((f32[2,512,256]{2,1,0:T(8,128)S(1)}, f32[2,512,256]{2,1,0:T(8,128)}, u32[]{:S(2)}, u32[]{:S(2)}) %collective-permute-start.1) | collective-permute-done | bytes 1048608 | tf_op jit(solution)/shard_map/ppermute | solution.py:12
  47.1 1.8 pad_maximum_fusion
  49.7 1.6 broadcast_in_dim.12
  51.3 39.8 %while.17 = (s32[]{:T(128)}, f32[2,512,512]{2,1,0:T(8,128)}, f32[2,256,256]{2,1,0:T(8,128)}, f32[256,256]{1,0:T(8,128)S(1)}, s32[]{:T(128)}, /*index=5*/s32[4,2]...) while((s32[]{:T(128)}, f32[2,512,512]{2,1,0:T(8,128)}, ...), condition=%wide.region_1.2_spmd.clone.clone, body=%wide.region_0.1_spmd.clone.clone.sunk | while | flops 3240755200 | bytes 23855492 | solution.py:88
  56.6 1.5 fusion.185
  58.1 1.5 convolution_subtract_fusion.7
  61.1 1.5 convolution_add_fusion.7
  62.6 1.5 fusion.188
  65.5 1.5 convolution_subtract_fusion.8
  67.0 2.4 fusion.189
  70.9 1.5 convolution_subtract_fusion.9
  73.9 1.5 convolution_add_fusion.8
  76.9 1.5 fusion.191
  79.8 1.7 add_bitcast_fusion.2
  81.6 1.5 maximum_add_fusion.3
  83.9 6.6 dynamic_update_slice.7
  91.2 2.4 slice.55
  93.6 2.3 collective-permute-start.2
  95.9 21.7 %collective-permute-done.2 = f32[2,512,256]{2,1,0:T(8,128)} collective-permute-done((f32[2,512,256]{2,1,0:T(8,128)}, f32[2,512,256]{2,1,0:T(8,128)}, u32[]{:S(2)}, u32[]{:S(2)}) %collective-permute-start.2) | collective-permute-done | bytes 1048608 | tf_op jit(solution)/shard_map/ppermute | solution.py:12
  119.9 83.8 %collective-permute-start.3 = (f32[2,256,256]{2,1,0:T(8,128)S(1)}, f32[2,256,256]{2,1,0:T(8,128)S(1)}, u32[]{:S(2)}, u32[]{:S(2)}) collective-permute-start(f32[2,256,256]{2,1,0:T(8,128)S(1)} %slice.75), channel_id=1, source_target_pairs={{0,32},{32,64},{64,96},{96,128},{128,160},{160,192},{192,224},{224... | collective-permute-start | bytes 1572872 | tf_op jit(solution)/shard_map/ppermute | solution.py:12
  203.8 481.6 %all-reduce.3.cloned.1.call-done = (f32[2,256,256]{2,1,0:T(8,128)}, f32[256,256]{1,0:T(8,128)}) async-done(((f32[2,256,256]{2,1,0:T(8,128)}, f32[256,256]{1,0:T(8,128)}), (f32[2,256,256]{2,1,0:T(8,128)}, f32[256,256]{1,0:T(8,128)})) %all-reduce.3.cloned.1.call-update) | async-done | bytes 786448 | tf_op jit(solution)/shard_map/psum | solution.py:93
  686.4 1.9 broadcast_divide_fusion
  (39 shorter events, 18.1 us)
Async XLA Ops:
  7.2 678.2 %all-reduce.3.cloned.1.call-start = ((), (), s32[]{:S(2)}) async-start(), calls=%async_computation | async-start | bytes 1572864 | tf_op jit(solution)/shard_map/psum | solution.py:93
  7.2 11.6 %collective-permute-start = (f32[2,256,256]{2,1,0:T(8,128)}, f32[2,256,256]{2,1,0:T(8,128)S(1)}, u32[]{:S(2)}, u32[]{:S(2)}) collective-permute-start(f32[2,256,256]{2,1,0:T(8,128)} %param.7), channel_id=1, source_target_pairs={{32,0},{64,32},{96,64},{128,96},{160,128},{192,160},{224,192},{256... | collective-permute-start | bytes 1572872 | tf_op jit(solution)/shard_map/ppermute | solution.py:12
  18.8 1.3 copy-start.7
  18.8 28.2 %collective-permute-start.1 = (f32[2,512,256]{2,1,0:T(8,128)S(1)}, f32[2,512,256]{2,1,0:T(8,128)}, u32[]{:S(2)}, u32[]{:S(2)}) collective-permute-start(f32[2,512,256]{2,1,0:T(8,128)S(1)} %constant_dynamic-update-slice_fusion), channel_id=1, source_target_pairs={{1,0},{2,1},{3,2},{4,3},{5,4},{6,5},{7,6},{8,7},{9,8},{10,9},{11,1... | collective-permute-start | bytes 3145736 | tf_op jit(solution)/shard_map/ppermute | solution.py:12
  48.8 2.5 copy-start
  48.9 2.5 copy-start.8
  78.4 3.2 copy-start.1
  83.1 0.8 copy-start.2
  91.1 4.7 copy-start.4
  91.2 26.4 %copy-start.3 = (f32[2,512,512]{2,1,0:T(8,128)S(1)}, f32[2,512,512]{2,1,0:T(8,128)}, u32[]{:S(2)}) copy-start(f32[2,512,512]{2,1,0:T(8,128)} %get-tuple-element.151) | copy-start | bytes 6291460
  93.6 23.9 %collective-permute-start.2 = (f32[2,512,256]{2,1,0:T(8,128)}, f32[2,512,256]{2,1,0:T(8,128)}, u32[]{:S(2)}, u32[]{:S(2)}) collective-permute-start(f32[2,512,256]{2,1,0:T(8,128)} %slice.55), channel_id=1, source_target_pairs={{0,1},{1,2},{2,3},{3,4},{4,5},{5,6},{6,7},{7,8},{8,9},{9,10},{10,1... | collective-permute-start | bytes 3145736 | tf_op jit(solution)/shard_map/ppermute | solution.py:12
  118.9 1.0 copy-start.5
  119.9 568.4 %copy-start.6 = (f32[2,512,256]{2,1,0:T(8,128)S(1)}, f32[2,512,256]{2,1,0:T(8,128)}, u32[]{:S(2)}) copy-start(f32[2,512,256]{2,1,0:T(8,128)} %copy-done.5) | copy-start | bytes 3145732
  119.9 568.4 %collective-permute-start.3 = (f32[2,256,256]{2,1,0:T(8,128)S(1)}, f32[2,256,256]{2,1,0:T(8,128)S(1)}, u32[]{:S(2)}, u32[]{:S(2)}) collective-permute-start(f32[2,256,256]{2,1,0:T(8,128)S(1)} %slice.75), channel_id=1, source_target_pairs={{0,32},{32,64},{64,96},{96,128},{128,160},{160,192},{192,224},{224... | collective-permute-start | bytes 1572872 | tf_op jit(solution)/shard_map/ppermute | solution.py:12
Sparse Core Ops, SparseCore 0:
  96.0 589.3 all-reduce.2
where the time goes:
time: 698 us; the launch traced here: 696 us
  waiting for transfers between devices  532 us (76%)
  starting transfers between devices  96.2 us (14%)
  matrix products  24.8 us (4%)
  local copies, waits for them, and re-layouts  15.1 us (2%)
  between operations  14.2 us (2%)
  other arithmetic  8.6 us (1%)
    psum x1, waiting for transfers between devices, on_device(): total_probe, total_illum = lax.psum((gprobe, illum), ('row', 'col'))  482 us
    ppermute x4, starting transfers between devices, passed_along(): return lax.ppermute(block, axis, route)  96.2 us
    ppermute x4, waiting for transfers between devices, passed_along(): return lax.ppermute(block, axis, route)  50.3 us
    dot_general x16, matrix products, matmul(): jnp.dot(left, right, precision=lax.Precision.HIGHEST, preferred_element_t...  24.8 us
  transfers between devices with their start and end apart: 5, of which 4 were waited for; matrix products, arithmetic and copies ran while one was open for 1% of the time, Pallas kernels for 0%

commit v1 on v0

v1 whole, which is shorter than its diff:
```python
import functools
import math

import jax
import jax.numpy as jnp
import ml_dtypes
import numpy as np
from jax import lax
from jax.experimental import pallas as pl
from jax.experimental.pallas import tpu as pltpu
from jax.sharding import PartitionSpec as P

MESH = pl.DeviceIdType.MESH
PS = 256
HALF = 128
CAP = 4
CHUNKS = 4
ROWS = PS // CHUNKS
PLANE = 16
OWNERS = 4
F32 = jnp.float32
BF16 = jnp.bfloat16


def split_bf16(table):
    high = table.astype(ml_dtypes.bfloat16)
    low = (table - high.astype(np.float64)).astype(ml_dtypes.bfloat16)
    return high, low


def constants():
    n = np.arange(HALF)
    angle = 2.0 * math.pi * ((n[:, None] * n[None, :]) % HALF) / HALF
    cos, sin = np.cos(angle) / 16.0, np.sin(angle) / 16.0
    matrix = np.block([[cos, -sin], [sin, cos]])
    high, low = split_bf16(matrix)
    high_t, low_t = split_bf16(matrix.T)
    tables = np.stack([high, low, high_t, low_t])
    turn = 2.0 * math.pi * n / PS
    tw = np.stack([np.cos(turn), -np.sin(turn)]).astype(np.float32)
    lane_tw = np.broadcast_to(tw[:, None, :], (2, 8, HALF)).copy()
    row_tw = np.broadcast_to(tw[:, :, None], (2, HALF, HALF)).copy()
    order = np.zeros((PS, PS), np.float32)
    lane = np.arange(PS)
    order[lane, (lane % 2) * HALF + lane // 2] = 1.0
    orders = np.stack([order, order.T]).astype(ml_dtypes.bfloat16)
    return tables, lane_tw, row_tw, orders


def dot(left, right):
    return jnp.dot(left, right, preferred_element_type=F32)


def halves(x):
    high = x.astype(BF16)
    return high, (x - high.astype(F32)).astype(BF16)


def kernel(
    rows_n,
    cols_n,
    obj, probe, counts, offs, count, tables, lane_tw, row_tw, order,
    out_obj, out_probe,
    own, ext, patch, turned, measured, sorted_counts, probe_v, tab, ltw, rtw, perm,
    y_hi, y_lo, spec, grad, gsum, from_out, shared, core_in, plane_in, depth_in, final,
    load_sem, in_send, in_recv, fwd_send, out_send, out_recv,
    core_send, core_recv, plane_send, plane_recv, depth_send, depth_recv,
    spread_send, spread_recv, gather_send, gather_recv, last_send, last_recv,
):
    row, col = lax.axis_index("row"), lax.axis_index("col")
    core = lax.rem(row, 2)
    x_lo = lax.rem(row // 2, 2)
    y = row // 4
    z = col // 2
    x_hi = lax.rem(col, 2)
    depth = cols_n // 2
    rank = y * 4 + x_hi * 2 + x_lo

    def on_plane(other):
        return ((other // 4) * 4 + lax.rem(other, 2) * 2 + core, z * 2 + lax.rem(other // 2, 2))

    def at_depth(other):
        return (row, other * 2 + x_hi)

    up, down = lax.rem(row + rows_n - 1, rows_n), lax.rem(row + 1, rows_n)
    left, right = lax.rem(col + cols_n - 1, cols_n), lax.rem(col + 1, cols_n)
    partner = (row + 1 - 2 * core, col)
    even = core == 0

    barrier = pltpu.get_barrier_semaphore()
    known = [(row, left), (row, right), (up, col), (down, col)]
    for other in known:
        pl.semaphore_signal(barrier, inc=1, device_id=other, device_id_type=MESH)

    @pl.when(even)
    def _():
        pl.semaphore_signal(barrier, inc=1, device_id=(up, left), device_id_type=MESH)

    @pl.when(jnp.logical_not(even))
    def _():
        pl.semaphore_signal(barrier, inc=1, device_id=(down, right), device_id_type=MESH)

    for step in range(1, PLANE):
        pl.semaphore_signal(
            barrier, inc=1, device_id=on_plane(lax.rem(rank + step, PLANE)), device_id_type=MESH
        )
    for step in range(1, depth):
        pl.semaphore_signal(
            barrier, inc=1, device_id=at_depth(lax.rem(z + step, depth)), device_id_type=MESH
        )

    loads = []
    for index, (src, dst) in enumerate(
        [
            (obj, own), (probe, probe_v), (counts, measured), (tables, tab),
            (lane_tw, ltw), (row_tw, rtw), (order, perm),
        ]
    ):
        load = pltpu.make_async_copy(src, dst, load_sem.at[index])
        load.start()
        loads.append(load)

    pl.semaphore_wait(barrier, 5 + PLANE - 1 + depth - 1)

    def halo_copy(slot, chunk, target):
        part = pl.ds(chunk * ROWS, ROWS)
        return pltpu.make_async_remote_copy(
            src_ref=obj.at[:, part, :],
            dst_ref=ext.at[slot, :, part, :],
            send_sem=in_send.at[slot, chunk],
            recv_sem=in_recv.at[slot, chunk],
            device_id=target,
            device_id_type=MESH,
        )

    def forward_copy(chunk):
        part = pl.ds(chunk * ROWS, ROWS)
        return pltpu.make_async_remote_copy(
            src_ref=ext.at[0, :, part, :],
            dst_ref=ext.at[2, :, part, :],
            send_sem=fwd_send.at[chunk],
            recv_sem=in_recv.at[2, chunk],
            device_id=partner,
            device_id_type=MESH,
        )

    for chunk in range(CHUNKS):
        halo_copy(0, chunk, (row, left)).start()
        halo_copy(1, chunk, (up, col)).start()

        @pl.when(even)
        def _():
            halo_copy(2, chunk, (up, left)).start()

    for load in loads:
        load.wait()

    def prepare(slot, carry):
        oy, ox = offs[0, 0, slot, 0], offs[0, 0, slot, 1]
        for part in range(2):
            plane = pltpu.roll(probe_v[part], oy, 0)
            turned[slot, part] = pltpu.roll(plane, ox, 1)
        rest = measured[0, 0, slot]
        total = None
        for _ in range(3):
            piece = rest.astype(BF16)
            rest = rest - piece.astype(F32)
            piece = dot(dot(perm[1], piece).astype(BF16), perm[0])
            total = piece if total is None else total + piece
        sorted_counts[slot] = total
        return carry

    lax.fori_loop(0, CAP, prepare, 0)
    gsum[...] = jnp.zeros_like(gsum)
    grad[...] = jnp.zeros_like(grad)

    tw_re, tw_im = ltw[0, 0:1, :], ltw[1, 0:1, :]

    for chunk in range(CHUNKS):
        first_row = chunk * ROWS
        part = pl.ds(first_row, ROWS)
        for slot in range(2):
            halo_copy(slot, chunk, partner).wait_recv()

        @pl.when(jnp.logical_not(even))
        def _():
            forward_copy(chunk).start()

        halo_copy(2, chunk, partner).wait_recv()

        def enter(slot, carry):
            oy, ox = offs[0, 0, slot, 0], offs[0, 0, slot, 1]
            row_at = lax.broadcasted_iota(jnp.int32, (ROWS, PS), 0) + first_row
            lane_at = lax.broadcasted_iota(jnp.int32, (ROWS, PS), 1)
            is_own_row = row_at >= oy
            is_own_col = lane_at >= ox
            low_ok = row < rows_n - 1
            right_ok = col < cols_n - 1
            use_own = jnp.logical_and(is_own_row, is_own_col)
            use_right = jnp.logical_and(jnp.logical_and(is_own_row, ~is_own_col), right_ok)
            use_low = jnp.logical_and(jnp.logical_and(~is_own_row, is_own_col), low_ok)
            use_diag = jnp.logical_and(
                jnp.logical_and(~is_own_row, ~is_own_col), jnp.logical_and(low_ok, right_ok)
            )
            planes = []
            for p in range(2):
                value = jnp.where(use_own, own[p, part, :], 0.0)
                value = jnp.where(use_right, ext[0, p, part, :], value)
                value = jnp.where(use_low, ext[1, p, part, :], value)
                value = jnp.where(use_diag, ext[2, p, part, :], value)
                patch[slot, p, part, :] = value
                planes.append(value)
            pr, pi = turned[slot, 0, part, :], turned[slot, 1, part, :]
            er = pr * planes[0] - pi * planes[1]
            ei = pr * planes[1] + pi * planes[0]
            ar, br, ai, bi = er[:, :HALF], er[:, HALF:], ei[:, :HALF], ei[:, HALF:]
            dr, di = ar - br, ai - bi
            sums = jnp.concatenate([ar + br, ai + bi], axis=1)
            diffs = jnp.concatenate([dr * tw_re - di * tw_im, dr * tw_im + di * tw_re], axis=1)
            at = pl.ds(pl.multiple_of(slot * ROWS, ROWS), ROWS)
            for parity, value in enumerate((sums, diffs)):
                high, low = halves(value)
                y_hi[parity, at, :] = high
                y_lo[parity, at, :] = low
            return carry

        lax.fori_loop(0, CAP, enter, 0)
        for parity in range(2):
            value = (
                dot(y_hi[parity], tab[0]) + dot(y_lo[parity], tab[0]) + dot(y_hi[parity], tab[1])
            )
            for slot in range(CAP):
                spec[slot, parity, part, :] = value[slot * ROWS : (slot + 1) * ROWS]

    def position(slot, carry):
        oy, ox = offs[0, 0, slot, 0], offs[0, 0, slot, 1]
        valid = jnp.where(count[0, 0] > slot, 1.0, 0.0).astype(F32)
        cr = jnp.concatenate([rtw[0], rtw[0]], axis=1)
        ci = jnp.concatenate([rtw[1], rtw[1]], axis=1)

        def block(where, half):
            piece = spec[slot, :, where, half * HALF : (half + 1) * HALF]
            return jnp.concatenate([piece[0], piece[1]], axis=1)

        top, bottom = pl.ds(0, HALF), pl.ds(HALF, HALF)
        ar, ai, br, bi = block(top, 0), block(top, 1), block(bottom, 0), block(bottom, 1)
        dr, di = ar - br, ai - bi
        sums = jnp.concatenate([ar + br, ai + bi], axis=0)
        diffs = jnp.concatenate([dr * cr - di * ci, dr * ci + di * cr], axis=0)
        backs = []
        for parity, value in enumerate((sums, diffs)):
            high, low = halves(value)
            wave = dot(tab[2], high) + dot(tab[2], low) + dot(tab[3], high)
            wr, wi = wave[:HALF], wave[HALF:]
            model = wr * wr + wi * wi + 0.5
            guess = pl.reciprocal(model, approx=True)
            guess = guess * (2.0 - model * guess)
            seen = sorted_counts[slot, parity * HALF : (parity + 1) * HALF, :]
            weight = valid - (valid * seen) * guess
            weighted = jnp.concatenate([weight * wr, weight * wi], axis=0)
            high, low = halves(weighted)
            backs.append(dot(tab[0], high) + dot(tab[0], low) + dot(tab[1], high))
        er, ei = backs[0][:HALF], backs[0][HALF:]
        dr, di = backs[1][:HALF], backs[1][HALF:]
        fr, fi = dr * cr + di * ci, di * cr - dr * ci
        vr = jnp.concatenate([er + fr, er - fr], axis=0)
        vi = jnp.concatenate([ei + fi, ei - fi], axis=0)
        ends = []
        for parity in range(2):
            lanes = slice(parity * HALF, (parity + 1) * HALF)
            high, low = halves(jnp.concatenate([vr[:, lanes], vi[:, lanes]], axis=1))
            ends.append(dot(high, tab[2]) + dot(low, tab[2]) + dot(high, tab[3]))
        er, ei = ends[0][:, :HALF], ends[0][:, HALF:]
        dr, di = ends[1][:, :HALF], ends[1][:, HALF:]
        fr, fi = dr * tw_re + di * tw_im, di * tw_re - dr * tw_im
        chi_r = jnp.concatenate([er + fr, er - fr], axis=1)
        chi_i = jnp.concatenate([ei + fi, ei - fi], axis=1)

        pr, pi = patch[slot, 0], patch[slot, 1]
        back_y, back_x = lax.rem(PS - oy, PS), lax.rem(PS - ox, PS)
        for p, value in enumerate(
            (
                pr * chi_r + pi * chi_i,
                pr * chi_i - pi * chi_r,
                valid * (pr * pr + pi * pi),
            )
        ):
            value = pltpu.roll(pltpu.roll(value, back_y, 0), back_x, 1)
            gsum[2 * p] += value[:, :HALF]
            gsum[2 * p + 1] += value[:, HALF:]

        qr, qi = turned[slot, 0], turned[slot, 1]
        is_own_row = lax.broadcasted_iota(jnp.int32, (PS, PS), 0) >= oy
        is_own_col = lax.broadcasted_iota(jnp.int32, (PS, PS), 1) >= ox
        for p, value in enumerate((qr * chi_r + qi * chi_i, qr * chi_i - qi * chi_r)):
            here = jnp.where(is_own_col, value, 0.0)
            there = value - here
            here_own = jnp.where(is_own_row, here, 0.0)
            there_own = jnp.where(is_own_row, there, 0.0)
            grad[0, p] += here_own
            grad[1, p] += there_own
            grad[2, p] += here - here_own
            grad[3, p] += there - there_own
        return carry

    lax.fori_loop(0, CAP, position, 0)

    mine = pl.ds(pl.multiple_of(core * HALF, HALF), HALF)
    other = pl.ds(pl.multiple_of((1 - core) * HALF, HALF), HALF)

    def remote(src, dst, send, recv, target):
        return pltpu.make_async_remote_copy(
            src_ref=src, dst_ref=dst, send_sem=send, recv_sem=recv,
            device_id=target, device_id_type=MESH,
        )

    core_copy = remote(gsum.at[:, other, :], core_in, core_send, core_recv, partner)
    core_copy.start()

    share_copy = remote(grad.at[3], shared, out_send.at[3], out_recv.at[3], partner)
    low_copy = remote(grad.at[2], from_out.at[1], out_send.at[1], out_recv.at[1], (down, col))
    right_copy = remote(grad.at[1], from_out.at[0], out_send.at[0], out_recv.at[0], (row, right))
    diag_copy = remote(grad.at[3], from_out.at[2], out_send.at[2], out_recv.at[2], (down, right))

    @pl.when(even)
    def _():
        share_copy.start()

    low_copy.start()

    @pl.when(even)
    def _():
        right_copy.start()

    @pl.when(jnp.logical_not(even))
    def _():
        diag_copy.start()

    core_copy.wait_recv()
    core_in[...] = core_in[...] + gsum[:, mine, :]

    def plane_copy(step):
        target = lax.rem(rank + step, PLANE)
        rows8 = pl.ds(pl.multiple_of(target * 8, 8), 8)
        return remote(
            core_in.at[:, rows8, :], plane_in.at[step],
            plane_send.at[step], plane_recv.at[step], on_plane(target),
        )

    for step in range(1, PLANE):
        plane_copy(step).start()

    @pl.when(jnp.logical_not(even))
    def _():
        share_copy.wait_recv()
        grad[1] = grad[1] + shared[...]
        right_copy.start()

    mine8 = pl.ds(pl.multiple_of(rank * 8, 8), 8)
    total = core_in[:, mine8, :]
    for step in range(1, PLANE):
        plane_copy(step).wait_recv()
        total = total + plane_in[step]
    plane_in[0] = total

    shift = lax.rem(rank, OWNERS)
    stride = depth // OWNERS

    def depth_step(part):
        return lax.rem(z - (part * stride + lax.rem(shift, stride)) + depth, depth)

    def depth_copies(part):
        step = depth_step(part)
        target = at_depth(part * stride + lax.rem(shift, stride))
        return (
            remote(
                plane_in.at[0, part], depth_in.at[step, 0],
                depth_send.at[part, 0], depth_recv.at[step, 0], target,
            ),
            remote(
                plane_in.at[0, 4 + part % 2], depth_in.at[step, 1],
                depth_send.at[part, 1], depth_recv.at[step, 1], target,
            ),
        )

    for part in range(OWNERS):
        @pl.when(depth_step(part) != 0)
        def _():
            for copy in depth_copies(part):
                copy.start()

    my_part = z // stride
    is_owner = lax.rem(z, stride) == lax.rem(shift, stride)
    place = pl.ds(pl.multiple_of(core * HALF + rank * 8, 8), 8)

    def spread_copy(step):
        return remote(
            final.at[my_part, place, :], final.at[my_part, place, :],
            spread_send.at[step], spread_recv.at[my_part], at_depth(lax.rem(z + step, depth)),
        )

    for part in range(OWNERS):
        @pl.when(depth_step(part) == 0)
        def _():
            gradient = plane_in[0, part]
            light = plane_in[0, 4 + part % 2]
            for other_step in range(1, depth):
                for which in range(2):
                    remote(
                        plane_in.at[0, part], depth_in.at[other_step, which],
                        depth_send.at[part, which], depth_recv.at[other_step, which], partner,
                    ).wait_recv()
                gradient = gradient + depth_in[other_step, 0]
                light = light + depth_in[other_step, 1]
            final[part, place, :] = gradient * lax.rsqrt(light + 1.0)

    @pl.when(is_owner)
    def _():
        for step in range(1, depth):
            spread_copy(step).start()

    for part in range(OWNERS):
        @pl.when(depth_step(part) != 0)
        def _():
            remote(
                final.at[part, place, :], final.at[part, place, :],
                spread_send.at[0], spread_recv.at[part], partner,
            ).wait_recv()

    def gather_copy(step):
        return remote(
            final.at[:, place, :], final.at[:, place, :],
            gather_send.at[step], gather_recv.at[step], on_plane(lax.rem(rank + step, PLANE)),
        )

    def gather_arrival(step):
        source = lax.rem(rank + PLANE - step, PLANE)
        at = pl.ds(pl.multiple_of(core * HALF + source * 8, 8), 8)
        return remote(
            final.at[:, at, :], final.at[:, at, :],
            gather_send.at[step], gather_recv.at[step], partner,
        )

    for step in range(1, PLANE):
        gather_copy(step).start()
    for step in range(1, PLANE):
        gather_arrival(step).wait_recv()
    last_copy = remote(final.at[:, mine, :], final.at[:, mine, :], last_send, last_recv, partner)
    last_arrival = remote(final.at[:, other, :], final.at[:, other, :], last_send, last_recv, partner)
    last_copy.start()

    low_copy.wait_recv()
    right_copy.wait_recv()
    above = jnp.where(row > 0, 1.0, 0.0).astype(F32)
    before = jnp.where(col > 0, 1.0, 0.0).astype(F32)
    tile = grad[0] + before * from_out[0] + above * from_out[1]
    out_obj[...] = tile

    @pl.when(even)
    def _():
        diag_copy.wait_recv()
        out_obj[...] = out_obj[...] + (above * before) * from_out[2]

    last_arrival.wait_recv()
    for p in range(2):
        out_probe[p, :, :HALF] = final[2 * p]
        out_probe[p, :, HALF:] = final[2 * p + 1]

    for chunk in range(CHUNKS):
        halo_copy(0, chunk, partner).wait_send()
        halo_copy(1, chunk, partner).wait_send()

        @pl.when(even)
        def _():
            halo_copy(2, chunk, partner).wait_send()

        @pl.when(jnp.logical_not(even))
        def _():
            forward_copy(chunk).wait_send()

    core_copy.wait_send()
    low_copy.wait_send()
    right_copy.wait_send()

    @pl.when(even)
    def _():
        share_copy.wait_send()

    @pl.when(jnp.logical_not(even))
    def _():
        diag_copy.wait_send()

    for step in range(1, PLANE):
        plane_copy(step).wait_send()
        gather_copy(step).wait_send()
    for part in range(OWNERS):
        @pl.when(depth_step(part) != 0)
        def _():
            for copy in depth_copies(part):
                copy.wait_send()

    @pl.when(is_owner)
    def _():
        for step in range(1, depth):
            spread_copy(step).wait_send()

    last_copy.wait_send()


def on_device(rows_n, cols_n, object_field, probe, counts_measured, offsets, slot_count):
    tables, lane_tw, row_tw, order = constants()
    depth = cols_n // 2
    any_spec = pl.BlockSpec(memory_space=pl.ANY)
    smem_spec = pl.BlockSpec(memory_space=pltpu.SMEM)
    vmem_spec = pl.BlockSpec(memory_space=pltpu.VMEM)
    tile = (2, PS, PS)
    dma = pltpu.SemaphoreType.DMA
    return pl.pallas_call(
        functools.partial(kernel, rows_n, cols_n),
        out_shape=(jax.ShapeDtypeStruct(tile, F32), jax.ShapeDtypeStruct(tile, F32)),
        in_specs=[any_spec, any_spec, any_spec, smem_spec, smem_spec] + [any_spec] * 4,
        out_specs=(vmem_spec, vmem_spec),
        scratch_shapes=[
            pltpu.VMEM(tile, F32),
            pltpu.VMEM((3,) + tile, F32),
            pltpu.VMEM((CAP,) + tile, F32),
            pltpu.VMEM((CAP,) + tile, F32),
            pltpu.VMEM((1, 1, CAP, PS, PS), F32),
            pltpu.VMEM((CAP, PS, PS), F32),
            pltpu.VMEM(tile, F32),
            pltpu.VMEM((4, PS, PS), BF16),
            pltpu.VMEM((2, 8, HALF), F32),
            pltpu.VMEM((2, HALF, HALF), F32),
            pltpu.VMEM((2, PS, PS), BF16),
            pltpu.VMEM((2, CAP * ROWS, PS), BF16),
            pltpu.VMEM((2, CAP * ROWS, PS), BF16),
            pltpu.VMEM((CAP, 2, PS, PS), F32),
            pltpu.VMEM((4,) + tile, F32),
            pltpu.VMEM((6, PS, HALF), F32),
            pltpu.VMEM((3,) + tile, F32),
            pltpu.VMEM(tile, F32),
            pltpu.VMEM((6, HALF, HALF), F32),
            pltpu.VMEM((PLANE, 6, 8, HALF), F32),
            pltpu.VMEM((depth, 2, 8, HALF), F32),
            pltpu.VMEM((4, PS, HALF), F32),
            dma((7,)),
            dma((3, CHUNKS)),
            dma((3, CHUNKS)),
            dma((CHUNKS,)),
            dma((4,)),
            dma((4,)),
            dma,
            dma,
            dma((PLANE,)),
            dma((PLANE,)),
            dma((OWNERS, 2)),
            dma((depth, 2)),
            dma((depth,)),
            dma((OWNERS,)),
            dma((PLANE,)),
            dma((PLANE,)),
            dma,
            dma,
        ],
        compiler_params=pltpu.CompilerParams(
            collective_id=0, has_side_effects=True, vmem_limit_bytes=48 << 20
        ),
        name="ptychography",
    )(
        object_field, probe, counts_measured, offsets, slot_count,
        jnp.asarray(tables), jnp.asarray(lane_tw), jnp.asarray(row_tw), jnp.asarray(order),
    )


def solution(mesh):
    rows_n, cols_n = mesh.shape["row"], mesh.shape["col"]
    return jax.shard_map(
        functools.partial(on_device, rows_n, cols_n),
        mesh=mesh,
        in_specs=(
            P(None, "row", "col"),
            P(),
            P("row", "col", None, None, None),
            P("row", "col", None, None),
            P("row", "col"),
        ),
        out_specs=(P(None, "row", "col"), P()),
        check_vma=False,
    )
```

time: 698 us -> 103 us (0.15)
  waiting for transfers between devices: 532 us -> 0 us
  starting transfers between devices: 96.2 us -> 0 us
  Pallas kernels: 0 us -> 92.4 us
  matrix products: 24.8 us -> 0 us
  between operations: 14.2 us -> 1.31 us
  other arithmetic: 8.6 us -> 0 us
    psum x1 -> x0, waiting for transfers between devices: 482 us -> none  [on_device(): total_probe, total_illum = lax.psum((gprobe, illum), ('row', 'col'))]
    ppermute x4 -> x0, starting transfers between devices: 96.2 us -> none  [passed_along(): return lax.ppermute(block, axis, route)]
    pallas_call x0 -> x1, Pallas kernels: none -> 92.4 us  [on_device(): pl.pallas_call(functools.partial(kernel, rows_n, cols_n), out_shape=(jax....]
    ppermute x4 -> x0, waiting for transfers between devices: 50.3 us -> none  [passed_along(): return lax.ppermute(block, axis, route)]
    dot_general x16 -> x0, matrix products: 24.8 us -> none  [matmul(): jnp.dot(left, right, precision=lax.Precision.HIGHEST, preferred_element_t...]
  transfers between devices with their start and end apart: 5 -> 0, of which waited for: 4 -> 0; matrix products, arithmetic and copies ran while one was open for 1% -> 0% of each run, Pallas kernels for 0% -> 0%
where the time goes in v1:
time: 103 us; the launch traced here: 102 us
  Pallas kernels  92.4 us (90%)
  local copies, waits for them, and re-layouts  8.59 us (8%)
  between operations  1.31 us (1%)
    pallas_call x1, Pallas kernels, on_device(): pl.pallas_call(functools.partial(kernel, rows_n, cols_n), out_shape=(jax....  92.4 us
    unnamed x19, local copies, waits for them, and re-layouts  8.59 us

profile of v1, /device:TPU:1, one launch (start us, length us, event | category | flops | bytes accessed | tf_op | source)
XLA Modules:
  0.0 102.3 jit_solution(17096921554256337214)
XLA Ops:
  0.6 0.0 copy-start.7
  1.3 0.0 copy-done.7
  1.3 0.1 copy.11.offs
  1.4 0.0 copy-start
  1.4 1.2 %copy-done = f32[1,1,4,256,256]{4,3,2,1,0:T(8,128)S(1)} copy-done((f32[1,1,4,256,256]{4,3,2,1,0:T(8,128)S(1)}, f32[1,1,4,256,256]{4,3,2,1,0:T(8,128)}, u32[]{:S(2)}) %copy-start) | copy-done | bytes 1048600
  2.6 0.0 copy-start.1
  2.6 1.0 %copy-done.1 = f32[2,256,256]{2,1,0:T(8,128)S(1)} copy-done((f32[2,256,256]{2,1,0:T(8,128)S(1)}, f32[2,256,256]{2,1,0:T(8,128)}, u32[]{:S(2)}) %copy-start.1) | copy-done | bytes 524312
  3.7 0.0 copy-start.2
  3.7 1.0 %copy-done.2 = f32[2,256,256]{2,1,0:T(8,128)S(1)} copy-done((f32[2,256,256]{2,1,0:T(8,128)S(1)}, f32[2,256,256]{2,1,0:T(8,128)}, u32[]{:S(2)}) %copy-start.2) | copy-done | bytes 524312
  4.7 0.0 copy-start.3
  4.7 1.0 %copy-done.3 = bf16[4,256,256]{2,1,0:T(8,128)(2,1)S(1)} copy-done((bf16[4,256,256]{2,1,0:T(8,128)(2,1)S(1)}, bf16[4,256,256]{2,1,0:T(8,128)(2,1)}, u32[]{:S(2)}) %copy-start.3) | copy-done | bytes 524312
  5.8 0.0 copy-start.4
  5.8 0.9 copy-done.4
  6.7 0.0 copy-start.5
  6.7 0.9 copy-done.5
  7.6 0.0 copy-start.6
  7.6 0.7 copy-done.6
  8.3 92.4 %ptychography.1 = (f32[2,256,256]{2,1,0:T(8,128)S(1)}, f32[2,256,256]{2,1,0:T(8,128)S(1)}) custom-call(f32[2,256,256]{2,1,0:T(8,128)S(1)} %copy-done.1, f32[2,256,256]{2,1,0:T(8,128)S(1)} %copy-done.2, f32[1,1,4,256,256]{4,3,2,1,0:T(8,128)S(1)} %copy-done, s32[1,1,4,2]{3,2,1,0:T(4,128)S(1)} %copy.11.offs, s32[1,1]{1,0:T(1,128)S(6)} %copy.14.count, ...), custom_call_target="tpu_custom_call" | custom-call | tf_op jit(solution)/shard_map/ptychography/pallas_call | solution.py:518
  100.7 0.8 copy.15
  101.5 0.8 copy.16
Async XLA Ops:
  0.6 0.7 copy-start.7
  1.4 1.2 %copy-start = (f32[1,1,4,256,256]{4,3,2,1,0:T(8,128)S(1)}, f32[1,1,4,256,256]{4,3,2,1,0:T(8,128)}, u32[]{:S(2)}) copy-start(f32[1,1,4,256,256]{4,3,2,1,0:T(8,128)} %counts.1) | copy-start | bytes 3145732
  2.6 1.0 %copy-start.1 = (f32[2,256,256]{2,1,0:T(8,128)S(1)}, f32[2,256,256]{2,1,0:T(8,128)}, u32[]{:S(2)}) copy-start(f32[2,256,256]{2,1,0:T(8,128)} %obj.1) | copy-start | bytes 1572868
  3.7 1.0 %copy-start.2 = (f32[2,256,256]{2,1,0:T(8,128)S(1)}, f32[2,256,256]{2,1,0:T(8,128)}, u32[]{:S(2)}) copy-start(f32[2,256,256]{2,1,0:T(8,128)} %probe.1) | copy-start | bytes 1572868
  4.7 1.0 %copy-start.3 = (bf16[4,256,256]{2,1,0:T(8,128)(2,1)S(1)}, bf16[4,256,256]{2,1,0:T(8,128)(2,1)}, u32[]{:S(2)}) copy-start(bf16[4,256,256]{2,1,0:T(8,128)(2,1)} %constant.8.clone.tables) | copy-start | bytes 1572868
  5.8 0.9 copy-start.4
  6.7 0.9 copy-start.5
  7.6 0.7 copy-start.6

commit v2 on v1

v2 whole, which is shorter than its diff:
```python
import functools
import math

import jax
import jax.numpy as jnp
import numpy as np
from jax import lax
from jax.experimental import pallas as pl
from jax.experimental.pallas import tpu as pltpu
from jax.sharding import PartitionSpec as P

MESH = pl.DeviceIdType.MESH
PS = 256
HALF = 128
CAP = 4
CHUNKS = 4
ROWS = PS // CHUNKS
PLANE = 16
NEAR = 4
F32 = jnp.float32
BF16 = jnp.bfloat16


def constants():
    n = np.arange(HALF)
    angle = 2.0 * math.pi * ((n[:, None] * n[None, :]) % HALF) / HALF
    cos, sin = np.cos(angle) / 16.0, np.sin(angle) / 16.0
    matrix = np.block([[cos, -sin], [sin, cos]])
    tables = np.stack([matrix, matrix.T]).astype(np.float32)
    turn = 2.0 * math.pi * n / PS
    tw = np.stack([np.cos(turn), -np.sin(turn)]).astype(np.float32)
    lane_tw = np.broadcast_to(tw[:, None, :], (2, 8, HALF)).copy()
    row_tw = np.broadcast_to(tw[:, :, None], (2, HALF, HALF)).copy()
    order = np.zeros((PS, PS), np.float32)
    lane = np.arange(PS)
    order[lane, (lane % 2) * HALF + lane // 2] = 1.0
    orders = np.stack([order, order.T])
    return np.concatenate([tables, orders]), lane_tw, row_tw


def dot(left, right):
    return jnp.dot(left, right, preferred_element_type=F32)


def halves(x):
    high = x.astype(BF16)
    return high, (x - high.astype(F32)).astype(BF16)


def kernel(
    rows_n,
    cols_n,
    obj, probe, counts, offs, count, tables, lane_tw, row_tw,
    out_obj, out_probe,
    own, ext, patch, turned, measured, sorted_counts, probe_v, made, tab, ltw, rtw, perm,
    y_hi, y_lo, spec, grad, gsum, lsum, from_out, shared, final,
    core_in, plane_in, near_in, far_in, core_light, plane_light, near_light, far_light,
    load_sem, in_send, in_recv, fwd_send, out_send, out_recv,
    core_send, core_recv, plane_send, plane_recv, near_send, near_recv, far_send, far_recv,
    gather_send, gather_recv, last_send, last_recv, store_sem,
):
    row, col = lax.axis_index("row"), lax.axis_index("col")
    core = lax.rem(row, 2)
    x_lo = lax.rem(row // 2, 2)
    y = row // 4
    z = col // 2
    x_hi = lax.rem(col, 2)
    rank = y * 4 + x_hi * 2 + x_lo

    def on_plane(other):
        return ((other // 4) * 4 + lax.rem(other, 2) * 2 + core, z * 2 + lax.rem(other // 2, 2))

    def at_depth(other):
        return (row, other * 2 + x_hi)

    group, member = z // NEAR, lax.rem(z, NEAR)

    def near(step):
        return group * NEAR + lax.rem(member + step, NEAR)

    def far(step):
        return lax.rem(group + step, NEAR) * NEAR + member

    up, down = lax.rem(row + rows_n - 1, rows_n), lax.rem(row + 1, rows_n)
    left, right = lax.rem(col + cols_n - 1, cols_n), lax.rem(col + 1, cols_n)
    partner = (row + 1 - 2 * core, col)
    even = core == 0

    barrier = pltpu.get_barrier_semaphore()
    known = [(row, left), (row, right), (up, col), (down, col)]
    for other in known:
        pl.semaphore_signal(barrier, inc=1, device_id=other, device_id_type=MESH)

    @pl.when(even)
    def _():
        pl.semaphore_signal(barrier, inc=1, device_id=(up, left), device_id_type=MESH)

    @pl.when(jnp.logical_not(even))
    def _():
        pl.semaphore_signal(barrier, inc=1, device_id=(down, right), device_id_type=MESH)

    for step in range(1, PLANE):
        pl.semaphore_signal(
            barrier, inc=1, device_id=on_plane(lax.rem(rank + step, PLANE)), device_id_type=MESH
        )
    for step in range(1, NEAR):
        for other in (near(step), far(step)):
            pl.semaphore_signal(barrier, inc=1, device_id=at_depth(other), device_id_type=MESH)

    loads = []
    for index, (src, dst) in enumerate(
        [
            (obj, own), (probe, probe_v), (counts, measured), (tables, made),
            (lane_tw, ltw), (row_tw, rtw),
        ]
    ):
        load = pltpu.make_async_copy(src, dst, load_sem.at[index])
        load.start()
        loads.append(load)

    pl.semaphore_wait(barrier, 5 + PLANE - 1 + 2 * (NEAR - 1))

    def halo_copy(slot, chunk, target):
        part = pl.ds(chunk * ROWS, ROWS)
        return pltpu.make_async_remote_copy(
            src_ref=obj.at[:, part, :],
            dst_ref=ext.at[slot, :, part, :],
            send_sem=in_send.at[slot, chunk],
            recv_sem=in_recv.at[slot, chunk],
            device_id=target,
            device_id_type=MESH,
        )

    def forward_copy(chunk):
        part = pl.ds(chunk * ROWS, ROWS)
        return pltpu.make_async_remote_copy(
            src_ref=ext.at[0, :, part, :],
            dst_ref=ext.at[2, :, part, :],
            send_sem=fwd_send.at[chunk],
            recv_sem=in_recv.at[2, chunk],
            device_id=partner,
            device_id_type=MESH,
        )

    for chunk in range(CHUNKS):
        halo_copy(0, chunk, (row, left)).start()
        halo_copy(1, chunk, (up, col)).start()

        @pl.when(even)
        def _():
            halo_copy(2, chunk, (up, left)).start()

    for load in loads:
        load.wait()

    for index in range(2):
        tab[2 * index], tab[2 * index + 1] = halves(made[index])
        perm[index] = made[2 + index].astype(BF16)

    def prepare(slot, carry):
        oy, ox = offs[0, 0, 0, slot], offs[0, 0, 1, slot]
        for part in range(2):
            plane = pltpu.roll(probe_v[part], oy, 0)
            turned[slot, part] = pltpu.roll(plane, ox, 1)
        rest = measured[0, 0, slot]
        total = None
        for _ in range(3):
            piece = rest.astype(BF16)
            rest = rest - piece.astype(F32)
            piece = dot(dot(perm[1], piece).astype(BF16), perm[0])
            total = piece if total is None else total + piece
        sorted_counts[slot] = total
        return carry

    lax.fori_loop(0, CAP, prepare, 0)
    gsum[...] = jnp.zeros_like(gsum)
    lsum[...] = jnp.zeros_like(lsum)
    grad[...] = jnp.zeros_like(grad)

    tw_re, tw_im = ltw[0, 0:1, :], ltw[1, 0:1, :]

    for chunk in range(CHUNKS):
        first_row = chunk * ROWS
        part = pl.ds(first_row, ROWS)
        for slot in range(2):
            halo_copy(slot, chunk, partner).wait_recv()

        @pl.when(jnp.logical_not(even))
        def _():
            forward_copy(chunk).start()

        halo_copy(2, chunk, partner).wait_recv()

        def enter(slot, carry):
            oy, ox = offs[0, 0, 0, slot], offs[0, 0, 1, slot]
            row_at = lax.broadcasted_iota(jnp.int32, (ROWS, PS), 0) + first_row
            lane_at = lax.broadcasted_iota(jnp.int32, (ROWS, PS), 1)
            is_own_row = row_at >= oy
            is_own_col = lane_at >= ox
            low_ok = row < rows_n - 1
            right_ok = col < cols_n - 1
            use_own = jnp.logical_and(is_own_row, is_own_col)
            use_right = jnp.logical_and(jnp.logical_and(is_own_row, ~is_own_col), right_ok)
            use_low = jnp.logical_and(jnp.logical_and(~is_own_row, is_own_col), low_ok)
            use_diag = jnp.logical_and(
                jnp.logical_and(~is_own_row, ~is_own_col), jnp.logical_and(low_ok, right_ok)
            )
            planes = []
            for p in range(2):
                value = jnp.where(use_own, own[p, part, :], 0.0)
                value = jnp.where(use_right, ext[0, p, part, :], value)
                value = jnp.where(use_low, ext[1, p, part, :], value)
                value = jnp.where(use_diag, ext[2, p, part, :], value)
                patch[slot, p, part, :] = value
                planes.append(value)
            pr, pi = turned[slot, 0, part, :], turned[slot, 1, part, :]
            er = pr * planes[0] - pi * planes[1]
            ei = pr * planes[1] + pi * planes[0]
            ar, br, ai, bi = er[:, :HALF], er[:, HALF:], ei[:, :HALF], ei[:, HALF:]
            dr, di = ar - br, ai - bi
            sums = jnp.concatenate([ar + br, ai + bi], axis=1)
            diffs = jnp.concatenate([dr * tw_re - di * tw_im, dr * tw_im + di * tw_re], axis=1)
            at = pl.ds(pl.multiple_of(slot * ROWS, ROWS), ROWS)
            for parity, value in enumerate((sums, diffs)):
                high, low = halves(value)
                y_hi[parity, at, :] = high
                y_lo[parity, at, :] = low
            return carry

        lax.fori_loop(0, CAP, enter, 0)
        for parity in range(2):
            value = (
                dot(y_hi[parity], tab[0]) + dot(y_lo[parity], tab[0]) + dot(y_hi[parity], tab[1])
            )
            for slot in range(CAP):
                spec[slot, parity, part, :] = value[slot * ROWS : (slot + 1) * ROWS]

    def position(slot, carry):
        oy, ox = offs[0, 0, 0, slot], offs[0, 0, 1, slot]
        valid = jnp.where(count[0, 0] > slot, 1.0, 0.0).astype(F32)
        cr = jnp.concatenate([rtw[0], rtw[0]], axis=1)
        ci = jnp.concatenate([rtw[1], rtw[1]], axis=1)

        def block(where, half):
            piece = spec[slot, :, where, half * HALF : (half + 1) * HALF]
            return jnp.concatenate([piece[0], piece[1]], axis=1)

        top, bottom = pl.ds(0, HALF), pl.ds(HALF, HALF)
        ar, ai, br, bi = block(top, 0), block(top, 1), block(bottom, 0), block(bottom, 1)
        dr, di = ar - br, ai - bi
        sums = jnp.concatenate([ar + br, ai + bi], axis=0)
        diffs = jnp.concatenate([dr * cr - di * ci, dr * ci + di * cr], axis=0)
        backs = []
        for parity, value in enumerate((sums, diffs)):
            high, low = halves(value)
            wave = dot(tab[2], high) + dot(tab[2], low) + dot(tab[3], high)
            wr, wi = wave[:HALF], wave[HALF:]
            model = wr * wr + wi * wi + 0.5
            guess = pl.reciprocal(model, approx=True)
            guess = guess * (2.0 - model * guess)
            seen = sorted_counts[slot, parity * HALF : (parity + 1) * HALF, :]
            weight = valid - (valid * seen) * guess
            weighted = jnp.concatenate([weight * wr, weight * wi], axis=0)
            high, low = halves(weighted)
            backs.append(dot(tab[0], high) + dot(tab[0], low) + dot(tab[1], high))
        er, ei = backs[0][:HALF], backs[0][HALF:]
        dr, di = backs[1][:HALF], backs[1][HALF:]
        fr, fi = dr * cr + di * ci, di * cr - dr * ci
        vr = jnp.concatenate([er + fr, er - fr], axis=0)
        vi = jnp.concatenate([ei + fi, ei - fi], axis=0)
        ends = []
        for parity in range(2):
            lanes = slice(parity * HALF, (parity + 1) * HALF)
            high, low = halves(jnp.concatenate([vr[:, lanes], vi[:, lanes]], axis=1))
            ends.append(dot(high, tab[2]) + dot(low, tab[2]) + dot(high, tab[3]))
        er, ei = ends[0][:, :HALF], ends[0][:, HALF:]
        dr, di = ends[1][:, :HALF], ends[1][:, HALF:]
        fr, fi = dr * tw_re + di * tw_im, di * tw_re - dr * tw_im
        chi_r = jnp.concatenate([er + fr, er - fr], axis=1)
        chi_i = jnp.concatenate([ei + fi, ei - fi], axis=1)

        pr, pi = patch[slot, 0], patch[slot, 1]
        back_y, back_x = lax.rem(PS - oy, PS), lax.rem(PS - ox, PS)
        for p, value in enumerate((pr * chi_r + pi * chi_i, pr * chi_i - pi * chi_r)):
            value = pltpu.roll(pltpu.roll(value, back_y, 0), back_x, 1)
            gsum[2 * p] += value[:, :HALF]
            gsum[2 * p + 1] += value[:, HALF:]

        spec[slot, 0] = chi_r
        spec[slot, 1] = chi_i
        return carry

    mine = pl.ds(pl.multiple_of(core * HALF, HALF), HALF)
    other = pl.ds(pl.multiple_of((1 - core) * HALF, HALF), HALF)
    mine8 = pl.ds(pl.multiple_of(rank * 8, 8), 8)
    place = pl.ds(pl.multiple_of(core * HALF + rank * 8, 8), 8)

    def remote(src, dst, send, recv, target):
        return pltpu.make_async_remote_copy(
            src_ref=src, dst_ref=dst, send_sem=send, recv_sem=recv,
            device_id=target, device_id_type=MESH,
        )

    class Sum:
        def __init__(self, full, core_in, plane_in, near_in, far_in, sems, which):
            self.full, self.core_in, self.plane_in = full, core_in, plane_in
            self.near_in, self.far_in = near_in, far_in
            (self.core_s, self.core_r, self.plane_s, self.plane_r,
             self.near_s, self.near_r, self.far_s, self.far_r) = sems
            self.which = which

        def core_copy(self):
            return remote(
                self.full.at[:, other, :], self.core_in,
                self.core_s.at[self.which], self.core_r.at[self.which], partner,
            )

        def plane_copy(self, step):
            target = lax.rem(rank + step, PLANE)
            rows8 = pl.ds(pl.multiple_of(target * 8, 8), 8)
            return remote(
                self.core_in.at[:, rows8, :], self.plane_in.at[step],
                self.plane_s.at[self.which, step], self.plane_r.at[self.which, step], on_plane(target),
            )

        def near_copy(self, step):
            return remote(
                self.near_in.at[member], self.near_in.at[member],
                self.near_s.at[self.which, step], self.near_r.at[self.which, step], at_depth(near(step)),
            )

        def near_arrival(self, step):
            at = lax.rem(member + NEAR - step, NEAR)
            return remote(
                self.near_in.at[at], self.near_in.at[at],
                self.near_s.at[self.which, step], self.near_r.at[self.which, step], partner,
            )

        def far_copy(self, step):
            return remote(
                self.far_in.at[group], self.far_in.at[group],
                self.far_s.at[self.which, step], self.far_r.at[self.which, step], at_depth(far(step)),
            )

        def far_arrival(self, step):
            at = lax.rem(group + NEAR - step, NEAR)
            return remote(
                self.far_in.at[at], self.far_in.at[at],
                self.far_s.at[self.which, step], self.far_r.at[self.which, step], partner,
            )

        def start(self):
            self.core_copy().start()

        def over_plane(self):
            self.core_copy().wait_recv()
            self.core_in[...] = self.core_in[...] + self.full[:, mine, :]
            for step in range(1, PLANE):
                self.plane_copy(step).start()

        def over_near(self):
            total = self.core_in[:, mine8, :]
            for step in range(1, PLANE):
                self.plane_copy(step).wait_recv()
                total = total + self.plane_in[step]
            self.near_in[member] = total
            for step in range(1, NEAR):
                self.near_copy(step).start()

        def over_far(self):
            for step in range(1, NEAR):
                self.near_arrival(step).wait_recv()
            self.far_in[group] = (self.near_in[0] + self.near_in[1]) + (self.near_in[2] + self.near_in[3])
            for step in range(1, NEAR):
                self.far_copy(step).start()

        def result(self):
            for step in range(1, NEAR):
                self.far_arrival(step).wait_recv()
            return (self.far_in[0] + self.far_in[1]) + (self.far_in[2] + self.far_in[3])

        def wait_sent(self):
            self.core_copy().wait_send()
            for step in range(1, PLANE):
                self.plane_copy(step).wait_send()
            for step in range(1, NEAR):
                self.near_copy(step).wait_send()
                self.far_copy(step).wait_send()

    sums = (core_send, core_recv, plane_send, plane_recv, near_send, near_recv, far_send, far_recv)
    light = Sum(lsum, core_light, plane_light, near_light, far_light, sums, 1)
    terms = Sum(gsum, core_in, plane_in, near_in, far_in, sums, 0)

    def brighten(slot, carry):
        oy, ox = offs[0, 0, 0, slot], offs[0, 0, 1, slot]
        valid = jnp.where(count[0, 0] > slot, 1.0, 0.0).astype(F32)
        pr, pi = patch[slot, 0], patch[slot, 1]
        back_y, back_x = lax.rem(PS - oy, PS), lax.rem(PS - ox, PS)
        value = pltpu.roll(pltpu.roll(valid * (pr * pr + pi * pi), back_y, 0), back_x, 1)
        lsum[0] += value[:, :HALF]
        lsum[1] += value[:, HALF:]
        return carry

    lax.fori_loop(0, CAP, brighten, 0)
    light.start()

    def step_of(slot, carry):
        position(slot, carry)

        @pl.when(slot == 1)
        def _():
            light.over_plane()

        return carry

    lax.fori_loop(0, CAP, step_of, 0)
    terms.start()

    def place_out(slot, carry):
        oy, ox = offs[0, 0, 0, slot], offs[0, 0, 1, slot]
        chi_r, chi_i = spec[slot, 0], spec[slot, 1]
        qr, qi = turned[slot, 0], turned[slot, 1]
        is_own_row = lax.broadcasted_iota(jnp.int32, (PS, PS), 0) >= oy
        is_own_col = lax.broadcasted_iota(jnp.int32, (PS, PS), 1) >= ox
        for p, value in enumerate((qr * chi_r + qi * chi_i, qr * chi_i - qi * chi_r)):
            here = jnp.where(is_own_col, value, 0.0)
            there = value - here
            here_own = jnp.where(is_own_row, here, 0.0)
            there_own = jnp.where(is_own_row, there, 0.0)
            grad[0, p] += here_own
            grad[1, p] += there_own
            grad[2, p] += here - here_own
            grad[3, p] += there - there_own
        return carry

    lax.fori_loop(0, CAP, place_out, 0)

    share_copy = remote(grad.at[3], shared, out_send.at[3, 0], out_recv.at[3, 0], partner)
    low_copy = remote(grad.at[2], from_out.at[1], out_send.at[1, 0], out_recv.at[1, 0], (down, col))

    def out_copy(tile, slot, piece, target):
        part = pl.ds(piece * ROWS, ROWS)
        return remote(
            grad.at[tile, :, part, :], from_out.at[slot, :, part, :],
            out_send.at[slot, piece], out_recv.at[slot, piece], target,
        )

    def right_copy(piece):
        return out_copy(1, 0, piece, (row, right))

    def diag_copy(piece):
        return out_copy(3, 2, piece, (down, right))

    inner = x_hi == 0

    def leave(who, right_pieces, diag_pieces):
        @pl.when(who)
        def _():
            for piece in diag_pieces:
                diag_copy(piece).start()
            for piece in right_pieces:
                right_copy(piece).start()

    outer_even = jnp.logical_and(jnp.logical_not(inner), even)
    outer_odd = jnp.logical_and(jnp.logical_not(inner), jnp.logical_not(even))
    inner_even = jnp.logical_and(inner, even)
    inner_odd = jnp.logical_and(inner, jnp.logical_not(even))

    @pl.when(even)
    def _():
        share_copy.start()

    leave(outer_even, (0, 1), ())
    leave(outer_odd, (), (0, 1))
    terms.over_plane()
    light.over_near()
    low_copy.start()

    @pl.when(jnp.logical_not(even))
    def _():
        share_copy.wait_recv()
        grad[1] = grad[1] + shared[...]

    leave(inner_even, range(4), ())
    leave(inner_odd, range(4), range(4))
    terms.over_near()
    light.over_far()
    leave(outer_even, (2,), ())
    leave(outer_odd, (), (2, 3))
    terms.over_far()
    leave(outer_even, (3,), ())
    leave(outer_odd, range(4), ())
    bright = light.result()
    scale = lax.rsqrt(bright + 1.0)
    total = terms.result()
    final[0, place, :] = total[0] * scale[0]
    final[1, place, :] = total[1] * scale[1]
    final[2, place, :] = total[2] * scale[0]
    final[3, place, :] = total[3] * scale[1]

    def gather_copy(step):
        return remote(
            final.at[:, place, :], final.at[:, place, :],
            gather_send.at[step], gather_recv.at[step], on_plane(lax.rem(rank + step, PLANE)),
        )

    def gather_arrival(step):
        source = lax.rem(rank + PLANE - step, PLANE)
        at = pl.ds(pl.multiple_of(core * HALF + source * 8, 8), 8)
        return remote(
            final.at[:, at, :], final.at[:, at, :],
            gather_send.at[step], gather_recv.at[step], partner,
        )

    def store_probe(where, first):
        return [
            pltpu.make_async_copy(
                final.at[block, where, :],
                out_probe.at[block // 2, where, (block % 2) * HALF : (block % 2 + 1) * HALF],
                store_sem.at[first + block],
            )
            for block in range(4)
        ]

    for step in range(1, PLANE):
        gather_copy(step).start()
    for step in range(1, PLANE):
        gather_arrival(step).wait_recv()
    last_copy = remote(final.at[:, mine, :], final.at[:, mine, :], last_send, last_recv, partner)
    last_arrival = remote(final.at[:, other, :], final.at[:, other, :], last_send, last_recv, partner)
    last_copy.start()
    stores = store_probe(mine, 0)
    for store in stores:
        store.start()

    low_copy.wait_recv()
    for piece in range(4):
        right_copy(piece).wait_recv()
    above = jnp.where(row > 0, 1.0, 0.0).astype(F32)
    before = jnp.where(col > 0, 1.0, 0.0).astype(F32)
    own[...] = grad[0] + before * from_out[0] + above * from_out[1]

    @pl.when(even)
    def _():
        for piece in range(4):
            diag_copy(piece).wait_recv()
        own[...] = own[...] + (above * before) * from_out[2]

    store_tile = pltpu.make_async_copy(own, out_obj, store_sem.at[8])
    store_tile.start()
    last_arrival.wait_recv()
    rest = store_probe(other, 4)
    for store in rest:
        store.start()

    for chunk in range(CHUNKS):
        halo_copy(0, chunk, partner).wait_send()
        halo_copy(1, chunk, partner).wait_send()

        @pl.when(even)
        def _():
            halo_copy(2, chunk, partner).wait_send()

        @pl.when(jnp.logical_not(even))
        def _():
            forward_copy(chunk).wait_send()

    light.wait_sent()
    terms.wait_sent()
    low_copy.wait_send()
    for piece in range(4):
        right_copy(piece).wait_send()

    @pl.when(even)
    def _():
        share_copy.wait_send()

    @pl.when(jnp.logical_not(even))
    def _():
        for piece in range(4):
            diag_copy(piece).wait_send()

    for step in range(1, PLANE):
        gather_copy(step).wait_send()
    last_copy.wait_send()
    for store in stores + rest:
        store.wait()
    store_tile.wait()


def on_device(rows_n, cols_n, object_field, probe, counts_measured, offsets, slot_count):
    tables, lane_tw, row_tw = constants()
    any_spec = pl.BlockSpec(memory_space=pltpu.HBM)
    smem_spec = pl.BlockSpec(memory_space=pltpu.SMEM)
    tile = (2, PS, PS)
    dma = pltpu.SemaphoreType.DMA
    return pl.pallas_call(
        functools.partial(kernel, rows_n, cols_n),
        out_shape=(jax.ShapeDtypeStruct(tile, F32), jax.ShapeDtypeStruct(tile, F32)),
        in_specs=[any_spec, any_spec, any_spec, smem_spec, smem_spec] + [any_spec] * 3,
        out_specs=(any_spec, any_spec),
        scratch_shapes=[
            pltpu.VMEM(tile, F32),
            pltpu.VMEM((3,) + tile, F32),
            pltpu.VMEM((CAP,) + tile, F32),
            pltpu.VMEM((CAP,) + tile, F32),
            pltpu.VMEM((1, 1, CAP, PS, PS), F32),
            pltpu.VMEM((CAP, PS, PS), F32),
            pltpu.VMEM(tile, F32),
            pltpu.VMEM((4, PS, PS), F32),
            pltpu.VMEM((4, PS, PS), BF16),
            pltpu.VMEM((2, 8, HALF), F32),
            pltpu.VMEM((2, HALF, HALF), F32),
            pltpu.VMEM((2, PS, PS), BF16),
            pltpu.VMEM((2, CAP * ROWS, PS), BF16),
            pltpu.VMEM((2, CAP * ROWS, PS), BF16),
            pltpu.VMEM((CAP, 2, PS, PS), F32),
            pltpu.VMEM((4,) + tile, F32),
            pltpu.VMEM((4, PS, HALF), F32),
            pltpu.VMEM((2, PS, HALF), F32),
            pltpu.VMEM((3,) + tile, F32),
            pltpu.VMEM(tile, F32),
            pltpu.VMEM((4, PS, HALF), F32),
            pltpu.VMEM((4, HALF, HALF), F32),
            pltpu.VMEM((PLANE, 4, 8, HALF), F32),
            pltpu.VMEM((NEAR, 4, 8, HALF), F32),
            pltpu.VMEM((NEAR, 4, 8, HALF), F32),
            pltpu.VMEM((2, HALF, HALF), F32),
            pltpu.VMEM((PLANE, 2, 8, HALF), F32),
            pltpu.VMEM((NEAR, 2, 8, HALF), F32),
            pltpu.VMEM((NEAR, 2, 8, HALF), F32),
            dma((6,)),
            dma((3, CHUNKS)),
            dma((3, CHUNKS)),
            dma((CHUNKS,)),
            dma((4, 4)),
            dma((4, 4)),
            dma((2,)),
            dma((2,)),
            dma((2, PLANE)),
            dma((2, PLANE)),
            dma((2, NEAR)),
            dma((2, NEAR)),
            dma((2, NEAR)),
            dma((2, NEAR)),
            dma((PLANE,)),
            dma((PLANE,)),
            dma,
            dma,
            dma((9,)),
        ],
        compiler_params=pltpu.CompilerParams(
            collective_id=0, has_side_effects=True, vmem_limit_bytes=60 << 20
        ),
        name="ptychography",
    )(
        object_field, probe, counts_measured, jnp.swapaxes(offsets, 2, 3), slot_count,
        jnp.asarray(tables), jnp.asarray(lane_tw), jnp.asarray(row_tw),
    )


def solution(mesh):
    rows_n, cols_n = mesh.shape["row"], mesh.shape["col"]
    return jax.shard_map(
        functools.partial(on_device, rows_n, cols_n),
        mesh=mesh,
        in_specs=(
            P(None, "row", "col"),
            P(),
            P("row", "col", None, None, None),
            P("row", "col", None, None),
            P("row", "col"),
        ),
        out_specs=(P(None, "row", "col"), P()),
        check_vma=False,
    )
```

time: 103 us -> 86.8 us (0.84)
  Pallas kernels: 92.4 us -> 82.7 us
  local copies, waits for them, and re-layouts: 8.59 us -> 2.72 us
    pallas_call x1, Pallas kernels: 92.4 us -> 82.7 us  [on_device(): pl.pallas_call(functools.partial(kernel, rows_n, cols_n), out_shape=(jax....]
    unnamed x19 -> x4, local copies, waits for them, and re-layouts: 8.59 us -> 2.72 us
where the time goes in v2:
time: 86.8 us; the launch traced here: 86.7 us
  Pallas kernels  82.7 us (95%)
  local copies, waits for them, and re-layouts  2.72 us (3%)
  between operations  1.29 us (1%)
    pallas_call x1, Pallas kernels, on_device(): pl.pallas_call(functools.partial(kernel, rows_n, cols_n), out_shape=(jax....  82.7 us
    unnamed x4, local copies, waits for them, and re-layouts  2.72 us

profile of v2, /device:TPU:1, one launch (start us, length us, event | category | flops | bytes accessed | tf_op | source)
XLA Modules:
  0.0 86.7 jit_solution(10141815097825655854)
XLA Ops:
  1.3 82.7 %ptychography.1 = (f32[2,256,256]{2,1,0:T(8,128)}, f32[2,256,256]{2,1,0:T(8,128)}) custom-call(f32[2,256,256]{2,1,0:T(8,128)} %obj.1, f32[2,256,256]{2,1,0:T(8,128)} %probe.1, f32[1,1,4,256,256]{4,3,2,1,0:T(8,128)} %counts.1, s32[1,1,2,4]{3,2,1,0:T(2,128)} %bitcast.1, s32[1,1]{1,0:T(1,128)S(6)} %copy.12.count, f32[4,256,256]{2,1,0:T(8,128)} %constant.6.clone.tables, ...), custom_call_target="tpu_custom_call" | custom-call | tf_op jit(solution)/shard_map/ptychography/pallas_call | solution.py:597
  83.9 0.0 copy-start
  83.9 1.9 %copy.13 = f32[2,256,256]{2,1,0:T(8,128)} copy(f32[2,256,256]{2,1,0:T(8,128)} %get-tuple-element.4) | data formatting | bytes 1048576
  85.9 0.0 copy-done
  85.9 0.8 copy.14
Async XLA Ops:
  83.9 1.9 %copy-start = (f32[2,256,256]{2,1,0:T(8,128)S(1)}, f32[2,256,256]{2,1,0:T(8,128)}, u32[]{:S(2)}) copy-start(f32[2,256,256]{2,1,0:T(8,128)} %get-tuple-element.5) | copy-start | bytes 1572868

commit v3 on v2

--- a/solution.py
+++ b/solution.py
@@ -53,7 +53,7 @@
     obj, probe, counts, offs, count, tables, lane_tw, row_tw,
     out_obj, out_probe,
     own, ext, patch, turned, measured, sorted_counts, probe_v, made, tab, ltw, rtw, perm,
-    y_hi, y_lo, spec, grad, gsum, lsum, from_out, shared, final,
+    y_hi, y_lo, spec, twice, bright_twice, grad, gsum, lsum, from_out, shared, final,
     core_in, plane_in, near_in, far_in, core_light, plane_light, near_light, far_light,
     load_sem, in_send, in_recv, fwd_send, out_send, out_recv,
     core_send, core_recv, plane_send, plane_recv, near_send, near_recv, far_send, far_recv,
@@ -213,6 +213,13 @@
                 value = jnp.where(use_diag, ext[2, p, part, :], value)
                 patch[slot, p, part, :] = value
                 planes.append(value)
+            valid = jnp.where(count[0, 0] > slot, 1.0, 0.0).astype(F32)
+            shine = valid * (planes[0] * planes[0] + planes[1] * planes[1])
+            shine = pltpu.roll(shine, lax.rem(PS - ox, PS), 1)
+            for h in range(2):
+                block = shine[:, h * HALF : (h + 1) * HALF]
+                bright_twice[slot, h, part, :] = block
+                bright_twice[slot, h, pl.ds(PS + first_row, ROWS), :] = block
             pr, pi = turned[slot, 0, part, :], turned[slot, 1, part, :]
             er = pr * planes[0] - pi * planes[1]
             ei = pr * planes[1] + pi * planes[0]
@@ -280,12 +287,14 @@
         chi_i = jnp.concatenate([ei + fi, ei - fi], axis=1)
 
         pr, pi = patch[slot, 0], patch[slot, 1]
-        back_y, back_x = lax.rem(PS - oy, PS), lax.rem(PS - ox, PS)
+        back_x = lax.rem(PS - ox, PS)
         for p, value in enumerate((pr * chi_r + pi * chi_i, pr * chi_i - pi * chi_r)):
-            value = pltpu.roll(pltpu.roll(value, back_y, 0), back_x, 1)
-            gsum[2 * p] += value[:, :HALF]
-            gsum[2 * p + 1] += value[:, HALF:]
-
+            value = pltpu.roll(value, back_x, 1)
+            for h in range(2):
+                block = value[:, h * HALF : (h + 1) * HALF]
+                twice[2 * p + h, :PS, :] = block
+                twice[2 * p + h, PS:, :] = block
+                gsum[2 * p + h] += twice[2 * p + h, pl.ds(oy, PS), :]
         spec[slot, 0] = chi_r
         spec[slot, 1] = chi_i
         return carry
@@ -392,28 +401,25 @@
     terms = Sum(gsum, core_in, plane_in, near_in, far_in, sums, 0)
 
     def brighten(slot, carry):
-        oy, ox = offs[0, 0, 0, slot], offs[0, 0, 1, slot]
-        valid = jnp.where(count[0, 0] > slot, 1.0, 0.0).astype(F32)
-        pr, pi = patch[slot, 0], patch[slot, 1]
-        back_y, back_x = lax.rem(PS - oy, PS), lax.rem(PS - ox, PS)
-        value = pltpu.roll(pltpu.roll(valid * (pr * pr + pi * pi), back_y, 0), back_x, 1)
-        lsum[0] += value[:, :HALF]
-        lsum[1] += value[:, HALF:]
+        oy = offs[0, 0, 0, slot]
+        for h in range(2):
+            lsum[h] += bright_twice[slot, h, pl.ds(oy, PS), :]
         return carry
 
     lax.fori_loop(0, CAP, brighten, 0)
     light.start()
 
     def step_of(slot, carry):
-        position(slot, carry)
-
-        @pl.when(slot == 1)
+        position(2 * slot, carry)
+        position(2 * slot + 1, carry)
+
+        @pl.when(slot == 0)
         def _():
             light.over_plane()
 
         return carry
 
-    lax.fori_loop(0, CAP, step_of, 0)
+    lax.fori_loop(0, CAP // 2, step_of, 0)
     terms.start()
 
     def place_out(slot, carry):
@@ -588,13 +594,34 @@
     store_tile.wait()
 
 
+def finish(tile, probe, out_tile, out_probe, tile_v, probe_v, in_sem, out_sem):
+    work = []
+    for piece in range(4):
+        part = pl.ds(piece * ROWS, ROWS)
+        for index, (src, held, dst) in enumerate(
+            ((tile, tile_v, out_tile), (probe, probe_v, out_probe))
+        ):
+            load = pltpu.make_async_copy(src.at[:, part, :], held.at[:, part, :], in_sem.at[index, piece])
+            load.start()
+            work.append((load, held.at[:, part, :], dst.at[:, part, :], out_sem.at[index, piece]))
+    stores = []
+    for load, src, dst, sem in work:
+        load.wait()
+        store = pltpu.make_async_copy(src, dst, sem)
+        store.start()
+        stores.append(store)
+    for store in stores:
+        store.wait()
+
+
 def on_device(rows_n, cols_n, object_field, probe, counts_measured, offsets, slot_count):
     tables, lane_tw, row_tw = constants()
     any_spec = pl.BlockSpec(memory_space=pltpu.HBM)
     smem_spec = pl.BlockSpec(memory_space=pltpu.SMEM)
     tile = (2, PS, PS)
     dma = pltpu.SemaphoreType.DMA
-    return pl.pallas_call(
+    shapes = (jax.ShapeDtypeStruct(tile, F32), jax.ShapeDtypeStruct(tile, F32))
+    results = pl.pallas_call(
         functools.partial(kernel, rows_n, cols_n),
         out_shape=(jax.ShapeDtypeStruct(tile, F32), jax.ShapeDtypeStruct(tile, F32)),
         in_specs=[any_spec, any_spec, any_spec, smem_spec, smem_spec] + [any_spec] * 3,
@@ -615,6 +642,8 @@
             pltpu.VMEM((2, CAP * ROWS, PS), BF16),
             pltpu.VMEM((2, CAP * ROWS, PS), BF16),
             pltpu.VMEM((CAP, 2, PS, PS), F32),
+            pltpu.VMEM((4, 2 * PS, HALF), F32),
+            pltpu.VMEM((CAP, 2, 2 * PS, HALF), F32),
             pltpu.VMEM((4,) + tile, F32),
             pltpu.VMEM((4, PS, HALF), F32),
             pltpu.VMEM((2, PS, HALF), F32),
@@ -657,6 +686,20 @@
         object_field, probe, counts_measured, jnp.swapaxes(offsets, 2, 3), slot_count,
         jnp.asarray(tables), jnp.asarray(lane_tw), jnp.asarray(row_tw),
     )
+    return pl.pallas_call(
+        finish,
+        out_shape=shapes,
+        in_specs=[any_spec, any_spec],
+        out_specs=(any_spec, any_spec),
+        scratch_shapes=[
+            pltpu.VMEM(tile, F32),
+            pltpu.VMEM(tile, F32),
+            dma((2, 4)),
+            dma((2, 4)),
+        ],
+        compiler_params=pltpu.CompilerParams(vmem_limit_bytes=60 << 20),
+        name="finish",
+    )(*results)
 
 
 def solution(mesh):

time: 86.8 us -> 85.2 us (0.982)
  local copies, waits for them, and re-layouts: 2.72 us -> 0 us
  Pallas kernels: 82.7 us -> 83.8 us
    unnamed x4 -> x0, local copies, waits for them, and re-layouts: 2.72 us -> none
    pallas_call x0 -> x1, Pallas kernels: none -> 2.09 us  [on_device(): pl.pallas_call(finish, out_shape=shapes, in_specs=[any_spec, any_spec], o...]
    pallas_call x1, Pallas kernels: 82.7 us -> 81.7 us  [on_device(): pl.pallas_call(functools.partial(kernel, rows_n, cols_n), out_shape=(jax....]
where the time goes in v3:
time: 85.2 us; the launch traced here: 85 us
  Pallas kernels  83.8 us (98%)
  between operations  1.29 us (2%)
    pallas_call x1, Pallas kernels, on_device(): pl.pallas_call(functools.partial(kernel, rows_n, cols_n), out_shape=(jax....  81.7 us
    pallas_call x1, Pallas kernels, on_device(): pl.pallas_call(finish, out_shape=shapes, in_specs=[any_spec, any_spec], o...  2.09 us

profile of v3, /device:TPU:1, one launch (start us, length us, event | category | flops | bytes accessed | tf_op | source)
XLA Modules:
  0.0 85.0 jit_solution(15100722591711605429)
XLA Ops:
  1.3 81.7 %ptychography.1 = (f32[2,256,256]{2,1,0:T(8,128)}, f32[2,256,256]{2,1,0:T(8,128)}) custom-call(f32[2,256,256]{2,1,0:T(8,128)} %obj.1, f32[2,256,256]{2,1,0:T(8,128)} %probe.1, f32[1,1,4,256,256]{4,3,2,1,0:T(8,128)} %counts.1, s32[1,1,2,4]{3,2,1,0:T(2,128)} %bitcast.1, s32[1,1]{1,0:T(1,128)S(6)} %copy.10.count, f32[4,256,256]{2,1,0:T(8,128)} %constant.6.clone.tables, ...), custom_call_target="tpu_custom_call" | custom-call | tf_op jit(solution)/shard_map/ptychography/pallas_call | solution.py:624
  82.9 2.1 %finish.1 = (f32[2,256,256]{2,1,0:T(8,128)}, f32[2,256,256]{2,1,0:T(8,128)}) custom-call(f32[2,256,256]{2,1,0:T(8,128)} %get-tuple-element.4.tile, f32[2,256,256]{2,1,0:T(8,128)} %get-tuple-element.5.probe), custom_call_target="tpu_custom_call" | custom-call | tf_op jit(solution)/shard_map/finish/pallas_call | solution.py:689

commit v4 on v3

--- a/solution.py
+++ b/solution.py
@@ -57,7 +57,7 @@
     core_in, plane_in, near_in, far_in, core_light, plane_light, near_light, far_light,
     load_sem, in_send, in_recv, fwd_send, out_send, out_recv,
     core_send, core_recv, plane_send, plane_recv, near_send, near_recv, far_send, far_recv,
-    gather_send, gather_recv, last_send, last_recv, store_sem,
+    gather_send, gather_recv, last_send, last_recv, store_sem, hello,
 ):
     row, col = lax.axis_index("row"), lax.axis_index("col")
     core = lax.rem(row, 2)
@@ -65,6 +65,7 @@
     y = row // 4
     z = col // 2
     x_hi = lax.rem(col, 2)
+    depth = cols_n // 2
     rank = y * 4 + x_hi * 2 + x_lo
 
     def on_plane(other):
@@ -104,8 +105,19 @@
             barrier, inc=1, device_id=on_plane(lax.rem(rank + step, PLANE)), device_id_type=MESH
         )
     for step in range(1, NEAR):
-        for other in (near(step), far(step)):
-            pl.semaphore_signal(barrier, inc=1, device_id=at_depth(other), device_id_type=MESH)
+        pl.semaphore_signal(barrier, inc=1, device_id=at_depth(near(step)), device_id_type=MESH)
+    first, last = member == 0, member == NEAR - 1
+    before_z, after_z = at_depth(lax.rem(z + depth - 1, depth)), at_depth(lax.rem(z + 1, depth))
+
+    @pl.when(first)
+    def _():
+        pl.semaphore_signal(barrier, inc=1, device_id=before_z, device_id_type=MESH)
+
+    @pl.when(last)
+    def _():
+        pl.semaphore_signal(barrier, inc=1, device_id=after_z, device_id_type=MESH)
+
+    edge = 1 - jnp.minimum(member * (NEAR - 1 - member), 1)
 
     loads = []
     for index, (src, dst) in enumerate(
@@ -118,7 +130,7 @@
         load.start()
         loads.append(load)
 
-    pl.semaphore_wait(barrier, 5 + PLANE - 1 + 2 * (NEAR - 1))
+    pl.semaphore_wait(barrier, 5 + PLANE - 1 + NEAR - 1 + edge)
 
     def halo_copy(slot, chunk, target):
         part = pl.ds(chunk * ROWS, ROWS)
@@ -149,6 +161,14 @@
         @pl.when(even)
         def _():
             halo_copy(2, chunk, (up, left)).start()
+
+    @pl.when(first)
+    def _():
+        pl.semaphore_signal(hello.at[0], inc=1, device_id=before_z, device_id_type=MESH)
+
+    @pl.when(last)
+    def _():
+        pl.semaphore_signal(hello.at[1], inc=1, device_id=after_z, device_id_type=MESH)
 
     for load in loads:
         load.wait()
@@ -178,6 +198,28 @@
     grad[...] = jnp.zeros_like(grad)
 
     tw_re, tw_im = ltw[0, 0:1, :], ltw[1, 0:1, :]
+
+    @pl.when(last)
+    def _():
+        pl.semaphore_wait(hello.at[0], 1)
+        for step in range(1, NEAR):
+            pl.semaphore_signal(hello.at[2], inc=1, device_id=at_depth(near(step)), device_id_type=MESH)
+
+    @pl.when(first)
+    def _():
+        pl.semaphore_wait(hello.at[1], 1)
+        for step in range(1, NEAR):
+            pl.semaphore_signal(hello.at[3], inc=1, device_id=at_depth(near(step)), device_id_type=MESH)
+
+    @pl.when(jnp.logical_not(last))
+    def _():
+        pl.semaphore_wait(hello.at[2], 1)
+
+    @pl.when(jnp.logical_not(first))
+    def _():
+        pl.semaphore_wait(hello.at[3], 1)
+
+    pl.semaphore_signal(hello.at[4], inc=1, device_id=at_depth(far(NEAR - 1)), device_id_type=MESH)
 
     for chunk in range(CHUNKS):
         first_row = chunk * ROWS
@@ -406,6 +448,7 @@
             lsum[h] += bright_twice[slot, h, pl.ds(oy, PS), :]
         return carry
 
+    pl.semaphore_wait(hello.at[4], 1)
     lax.fori_loop(0, CAP, brighten, 0)
     light.start()
 
@@ -677,6 +720,7 @@
             dma,
             dma,
             dma((9,)),
+            pltpu.SemaphoreType.REGULAR((5,)),
         ],
         compiler_params=pltpu.CompilerParams(
             collective_id=0, has_side_effects=True, vmem_limit_bytes=60 << 20

time: 85.2 us -> 83.1 us (0.975)
  Pallas kernels: 83.8 us -> 81.6 us
    pallas_call x1, Pallas kernels: 81.7 us -> 79.5 us  [on_device(): pl.pallas_call(functools.partial(kernel, rows_n, cols_n), out_shape=(jax....]
where the time goes in v4:
time: 83.1 us; the launch traced here: 82.9 us
  Pallas kernels  81.6 us (98%)
  between operations  1.29 us (2%)
    pallas_call x1, Pallas kernels, on_device(): pl.pallas_call(functools.partial(kernel, rows_n, cols_n), out_shape=(jax....  79.5 us
    pallas_call x1, Pallas kernels, on_device(): pl.pallas_call(finish, out_shape=shapes, in_specs=[any_spec, any_spec], o...  2.09 us

profile of v4, /device:TPU:1, one launch (start us, length us, event | category | flops | bytes accessed | tf_op | source)
XLA Modules:
  0.0 82.9 jit_solution(15798807124576626539)
XLA Ops:
  1.3 79.5 %ptychography.1 = (f32[2,256,256]{2,1,0:T(8,128)}, f32[2,256,256]{2,1,0:T(8,128)}) custom-call(f32[2,256,256]{2,1,0:T(8,128)} %obj.1, f32[2,256,256]{2,1,0:T(8,128)} %probe.1, f32[1,1,4,256,256]{4,3,2,1,0:T(8,128)} %counts.1, s32[1,1,2,4]{3,2,1,0:T(2,128)} %bitcast.1, s32[1,1]{1,0:T(1,128)S(6)} %copy.10.count, f32[4,256,256]{2,1,0:T(8,128)} %constant.6.clone.tables, ...), custom_call_target="tpu_custom_call" | custom-call | tf_op jit(solution)/shard_map/ptychography/pallas_call | solution.py:667
  80.8 2.1 %finish.1 = (f32[2,256,256]{2,1,0:T(8,128)}, f32[2,256,256]{2,1,0:T(8,128)}) custom-call(f32[2,256,256]{2,1,0:T(8,128)} %get-tuple-element.4.tile, f32[2,256,256]{2,1,0:T(8,128)} %get-tuple-element.5.probe), custom_call_target="tpu_custom_call" | custom-call | tf_op jit(solution)/shard_map/finish/pallas_call | solution.py:733

commit v5 on v4

--- a/solution.py
+++ b/solution.py
@@ -13,8 +13,9 @@
 PS = 256
 HALF = 128
 CAP = 4
-CHUNKS = 4
+CHUNKS = 8
 ROWS = PS // CHUNKS
+PIECE = PS // 4
 PLANE = 16
 NEAR = 4
 F32 = jnp.float32
@@ -488,7 +489,7 @@
     low_copy = remote(grad.at[2], from_out.at[1], out_send.at[1, 0], out_recv.at[1, 0], (down, col))
 
     def out_copy(tile, slot, piece, target):
-        part = pl.ds(piece * ROWS, ROWS)
+        part = pl.ds(piece * PIECE, PIECE)
         return remote(
             grad.at[tile, :, part, :], from_out.at[slot, :, part, :],
             out_send.at[slot, piece], out_recv.at[slot, piece], target,
@@ -640,7 +641,7 @@
 def finish(tile, probe, out_tile, out_probe, tile_v, probe_v, in_sem, out_sem):
     work = []
     for piece in range(4):
-        part = pl.ds(piece * ROWS, ROWS)
+        part = pl.ds(piece * PIECE, PIECE)
         for index, (src, held, dst) in enumerate(
             ((tile, tile_v, out_tile), (probe, probe_v, out_probe))
         ):

time: 83.1 us -> 82.5 us (level)
  no operation moved by 1% of the time
where the time goes in v5:
time: 82.5 us; the launch traced here: 82.3 us
  Pallas kernels  81 us (98%)
  between operations  1.29 us (2%)
    pallas_call x1, Pallas kernels, on_device(): pl.pallas_call(functools.partial(kernel, rows_n, cols_n), out_shape=(jax....  78.9 us
    pallas_call x1, Pallas kernels, on_device(): pl.pallas_call(finish, out_shape=shapes, in_specs=[any_spec, any_spec], o...  2.09 us

profile of v5, /device:TPU:1, one launch (start us, length us, event | category | flops | bytes accessed | tf_op | source)
XLA Modules:
  0.0 82.3 jit_solution(16950274737494572261)
XLA Ops:
  1.3 78.9 %ptychography.1 = (f32[2,256,256]{2,1,0:T(8,128)}, f32[2,256,256]{2,1,0:T(8,128)}) custom-call(f32[2,256,256]{2,1,0:T(8,128)} %obj.1, f32[2,256,256]{2,1,0:T(8,128)} %probe.1, f32[1,1,4,256,256]{4,3,2,1,0:T(8,128)} %counts.1, s32[1,1,2,4]{3,2,1,0:T(2,128)} %bitcast.1, s32[1,1]{1,0:T(1,128)S(6)} %copy.10.count, f32[4,256,256]{2,1,0:T(8,128)} %constant.6.clone.tables, ...), custom_call_target="tpu_custom_call" | custom-call | tf_op jit(solution)/shard_map/ptychography/pallas_call | solution.py:668
  80.2 2.1 %finish.1 = (f32[2,256,256]{2,1,0:T(8,128)}, f32[2,256,256]{2,1,0:T(8,128)}) custom-call(f32[2,256,256]{2,1,0:T(8,128)} %get-tuple-element.4.tile, f32[2,256,256]{2,1,0:T(8,128)} %get-tuple-element.5.probe), custom_call_target="tpu_custom_call" | custom-call | tf_op jit(solution)/shard_map/finish/pallas_call | solution.py:734
